TPU v7x, 32 devices: a whole 2x2x4 slice. The times are simulated.
32 devices in a mesh: groups: 2 (over y), space: 8 (over z, x), heads: 2 (over core).
Axes of the slice: x: 2, y: 2, z: 4, core: 2. Of those that a mesh axis runs over, the one named last changes fastest.
Arguments:
- queries: bfloat16 [2400, 1536], P(('groups', 'space'), 'heads'), parts along dimension 0, may hold values from -16 to 16
- latent_keys: bfloat16 [2400, 1536], P(('groups', 'space'), 'heads'), parts along dimension 0, may hold values from -9 to 9
- latent_values: bfloat16 [2400, 1536], P(('groups', 'space'), 'heads'), parts along dimension 0, may hold values from -6 to 6
- prompt: bfloat16 [512, 3072], P('groups'), parts along dimension 0, may hold values from -44 to 44
- key_weight: bfloat16 [3072, 1536], P('space', 'heads'), may hold values from -0.15625 to 0.15625
- value_weight: bfloat16 [3072, 1536], P('space', 'heads'), may hold values from -0.15625 to 0.15625
- out_weight: bfloat16 [1536, 3072], P('heads', 'space'), may hold values from -0.21875 to 0.21875
- tile_owner: int32 [16], P('groups'), parts along dimension 0, may hold values from 0 to 7, as said below
Outputs:
- block_output: bfloat16 [2400, 3072], P(('groups', 'space'), 'heads'), parts along dimension 0
There are 2 independent parts, one for each index of `groups`. A program takes and returns all parts, laid end to end along the dimension named above; an argument that names none is the same for every part. Nothing has to cross between parts.
Inputs may be any that keep to these rules, and one draw needn't show every extreme that they name: `tile_owner`: tile t = i * 2 + j of the 4 x 2 grid is held by slot a * 2 + b, with a = (i + r) mod 4 or a = (3 - i + r) mod 4 for one r, and b = j or b = 1 - j; r and each of the two alternatives are the same for all tiles.
All inputs are finite; a program needn't handle non-finite values.
Results may differ from a plain program's by a relative error of at most 0.0081.
Values may be sent and summed in bfloat16 or wider, within the bound.
A program may use at most 64 MiB of HBM per device.

v0:
```python
import jax
import jax.numpy as jnp
from jax import lax
from jax.sharding import PartitionSpec as P

HD = 128
RT = 16
RH = 56
TILE = 5


rope_theta = 256.0
eps_norm = 1e-06
masked_score = -1e30


def shifted(value, axis, steps):
    count = lax.axis_size(axis)
    pairs = [(source, (source + steps) % count) for source in range(count)]
    return lax.ppermute(value, axis, pairs)


def rope_tables(frame_pos, height_pos, width_pos):
    pairs_time = jnp.arange(RT // 2, dtype=jnp.float32)
    pairs_space = jnp.arange(RH // 2, dtype=jnp.float32)
    freq_time = rope_theta ** (-2.0 * pairs_time / RT)
    freq_space = rope_theta ** (-2.0 * pairs_space / RH)
    angles = jnp.concatenate(
        [
            frame_pos[:, None] * freq_time[None, :],
            height_pos[:, None] * freq_space[None, :],
            width_pos[:, None] * freq_space[None, :],
        ],
        axis=1,
    )
    return (jnp.cos(angles), jnp.sin(angles))


def rotate(stacked, cosine, sine_table):
    row_count = stacked.shape[0]
    head_total = stacked.shape[1]
    paired = stacked.reshape(row_count, head_total, HD // 2, 2)
    even_part = paired[..., 0]
    odd_part = paired[..., 1]
    cos_rows = cosine[:, None, :]
    sin_rows = sine_table[:, None, :]
    turned = jnp.stack(
        [even_part * cos_rows - odd_part * sin_rows, even_part * sin_rows + odd_part * cos_rows],
        axis=-1,
    )
    return turned.reshape(row_count, head_total * HD)


def normalize_keys(summed, head_total):
    row_count = summed.shape[0]
    half_width = summed.shape[1] // 2
    key_part = summed[:, :half_width].reshape(row_count, head_total, HD)
    key_part = key_part * lax.rsqrt(
        jnp.mean(key_part * key_part, axis=-1, keepdims=True) + eps_norm
    )
    return jnp.concatenate(
        [key_part.reshape(row_count, half_width), summed[:, half_width:]], axis=1
    ).astype(jnp.bfloat16)


def body(
    queries, latent_keys, latent_values, prompt, key_weight, value_weight, out_weight, tile_owner
):
    spaces = lax.axis_size("space")
    device = lax.axis_index("space")
    grid_h = min(8, spaces // 2)
    grid_w = spaces // grid_h
    tok_rows = queries.shape[0]
    head_width = queries.shape[1]
    head_count = head_width // HD
    tile_total = tile_owner.shape[0]
    tile_index = jnp.arange(tile_total, dtype=jnp.int32)
    own_tile = jnp.sum(jnp.where(tile_owner == device, tile_index, 0))
    tile_row = own_tile // grid_w
    tile_col = own_tile % grid_w
    anchor_slot = tile_owner[0]
    right_slot = tile_owner[min(1, tile_total - 1)]
    lower_slot = tile_owner[min(grid_w, tile_total - 1)]
    col_sign = jnp.where(right_slot % grid_w - anchor_slot % grid_w == -1, -1, 1)
    row_sign = jnp.where((lower_slot // grid_w - anchor_slot // grid_w) % grid_h == 1, 1, -1)
    cell_index = jnp.arange(tok_rows, dtype=jnp.int32)
    frame_pos = (cell_index // (TILE * TILE)).astype(jnp.float32)
    height_pos = (tile_row * TILE + cell_index // TILE % TILE).astype(jnp.float32)
    width_pos = (tile_col * TILE + cell_index % TILE).astype(jnp.float32)
    cosine, sine_table = rope_tables(frame_pos, height_pos, width_pos)
    query_rot = rotate(
        queries.astype(jnp.float32).reshape(tok_rows, head_count, HD), cosine, sine_table
    ).astype(jnp.bfloat16)
    key_rot = rotate(
        latent_keys.astype(jnp.float32).reshape(tok_rows, head_count, HD), cosine, sine_table
    ).astype(jnp.bfloat16)
    width_rows = key_weight.shape[0]
    text_cols = lax.dynamic_slice_in_dim(prompt, device * width_rows, width_rows, 1)
    both_weights = jnp.concatenate([key_weight, value_weight], axis=1)
    partial_text = jnp.dot(text_cols, both_weights, preferred_element_type=jnp.float32)
    summed_text = lax.psum(partial_text, "space")
    text_kv = normalize_keys(summed_text, head_count)
    kv_own = jnp.concatenate([key_rot, latent_values], axis=1)
    blocks = []
    valid_parts = []
    for row_step in (-1, 0, 1):
        for col_step in (-1, 0, 1):
            if row_step == 0 and col_step == 0:
                fetched = kv_own
            else:
                fetched = shifted(kv_own, "space", -(row_step * grid_w + col_step))
            near_row = tile_row + row_sign * row_step
            near_col = tile_col + col_sign * col_step
            inside = (near_row >= 0) & (near_row < grid_h) & (near_col >= 0) & (near_col < grid_w)
            blocks.append(fetched)
            valid_parts.append(jnp.zeros((tok_rows,), jnp.int32) + inside.astype(jnp.int32))
    blocks.append(text_kv)
    valid_parts.append(jnp.ones((text_kv.shape[0],), jnp.int32))
    keys_all = jnp.concatenate(blocks, axis=0)
    key_valid = jnp.concatenate(valid_parts, axis=0)
    score_scale = HD ** (-0.5)
    head_outputs = []
    for head_index in range(head_count):
        head_start = head_index * HD
        query_slice = query_rot[:, head_start : head_start + HD]
        key_slice = keys_all[:, head_start : head_start + HD]
        value_slice = keys_all[:, head_width + head_start : head_width + head_start + HD]
        scores = (
            lax.dot_general(
                query_slice, key_slice, (((1,), (1,)), ((), ())), preferred_element_type=jnp.float32
            )
            * score_scale
        )
        scores = jnp.where(key_valid[None, :] > 0, scores, masked_score)
        top_score = jnp.max(scores, axis=-1, keepdims=True)
        exponent = jnp.exp(scores - top_score)
        weights = (exponent / jnp.sum(exponent, axis=-1, keepdims=True)).astype(jnp.bfloat16)
        head_outputs.append(
            jnp.dot(weights, value_slice, preferred_element_type=jnp.float32).astype(jnp.bfloat16)
        )
    attended = jnp.concatenate(head_outputs, axis=1)
    partial_out = jnp.dot(
        attended,
        lax.all_gather(out_weight, "space", axis=1, tiled=True),
        preferred_element_type=jnp.float32,
    )
    summed_out = lax.psum_scatter(
        partial_out.astype(jnp.bfloat16), "heads", scatter_dimension=1, tiled=True
    )
    return summed_out


def solution(mesh):
    in_specs = (
        P(("groups", "space"), "heads"),
        P(("groups", "space"), "heads"),
        P(("groups", "space"), "heads"),
        P("groups", None),
        P("space", "heads"),
        P("space", "heads"),
        P("heads", "space"),
        P("groups"),
    )
    out_specs = P(("groups", "space"), "heads")
    return jax.shard_map(body, mesh=mesh, in_specs=in_specs, out_specs=out_specs, check_vma=False)
```

profile of v0, /device:TPU:0, one launch (start us, length us, event | category | flops | bytes accessed | tf_op | source)
XLA Modules:
  0.0 252.2 jit_solution(18399292161967376809)
XLA Ops:
  6.6 1.4 copy-done
  7.9 3.0 %fusion.6 = f32[256,1536]{1,0:T(8,128)} fusion(bf16[384,768]{1,0:T(8,128)(2,1)} %param.13, bf16[384,768]{1,0:T(8,128)(2,1)} %param.12, bf16[256,3072]{1,0:T(8,128)(2,1)S(1)} %copy-done, s32[]{:T(128)S(6)} %select_n.110), kind=kOutput, calls=%fused_computation.13 | convolution fusion | flops 304349184 | bytes 2949124 | tf_op jit(solution)/shard_map/dot_general | solution.py:100
  15.7 2.0 copy.10
  17.7 1.6 reshape.202
  19.7 2.7 %subtract_convert_fusion.1 = (bf16[150,6,64,1]{0,3,2,1:T(2,128)(2,1)S(1)}, bf16[150,6,64,1]{0,3,2,1:T(2,128)(2,1)}, bf16[150,6,64,1]{0,3,2,1:T(2,128)(2,1)S(1)}, bf16[150,6,64,1]{0,3,2,1:T(2,128)(2,1)S(1)}) fusion(f32[150,6,64,2]{0,3,2,1:T(2,128)S(1)} %reshape.201, f32[150,64]{0,1:T(8,128)S(1)} %get-tuple-element.12, f32[150,64]{0,1:T(8,128)S(1)} %get-tuple-element.11, ...), kind=kLoop, calls=%fused_computation.69 | loop fusion | flops 921600 | bytes 1459200 | tf_op jit(solution)/shard_map/convert.7
  24.0 1.7 pad_maximum_fusion.1
  25.7 4.0 %collective-permute-start = (bf16[150,1536]{1,0:T(8,128)(2,1)}, bf16[150,1536]{1,0:T(8,128)(2,1)}, u32[]{:S(2)}, u32[]{:S(2)}) collective-permute-start(bf16[150,1536]{1,0:T(8,128)(2,1)} %pad_maximum_fusion.1), channel_id=1, source_target_pairs={{0,6},{2,8},{4,10},{6,12},{8,14},{10,0},{12,2},{14,4},{1,7},{3,9},... | collective-permute-start | bytes 1382408 | tf_op jit(solution)/shard_map/ppermute | solution.py:20
  29.7 1.6 collective-permute-start.1
  31.3 1.5 collective-permute-start.2
  32.8 3.2 %collective-permute-start.3 = (bf16[150,1536]{1,0:T(8,128)(2,1)}, bf16[150,1536]{1,0:T(8,128)(2,1)}, u32[]{:S(2)}, u32[]{:S(2)}) collective-permute-start(bf16[150,1536]{1,0:T(8,128)(2,1)} %pad_maximum_fusion.1), channel_id=1, source_target_pairs={{0,14},{2,0},{4,2},{6,4},{8,6},{10,8},{12,10},{14,12},{1,15},{3,1}... | collective-permute-start | bytes 1382408 | tf_op jit(solution)/shard_map/ppermute | solution.py:20
  43.3 2.0 pad_maximum_fusion.2
  46.6 91.5 %all-reduce.2.cloned.1.call-done = f32[256,1536]{1,0:T(8,128)} async-done(((f32[256,1536]{1,0:T(8,128)}), f32[256,1536]{1,0:T(8,128)}) %all-reduce.2.cloned.1.call-update) | async-done | bytes 1572880 | tf_op jit(solution)/shard_map/psum | solution.py:101
  141.2 3.0 %collective-permute-start.5 = (bf16[150,1536]{1,0:T(8,128)(2,1)}, bf16[150,1536]{1,0:T(8,128)(2,1)S(1)}, u32[]{:S(2)}, u32[]{:S(2)}) collective-permute-start(bf16[150,1536]{1,0:T(8,128)(2,1)} %pad_maximum_fusion.1), channel_id=1, source_target_pairs={{0,10},{2,12},{4,14},{6,0},{8,2},{10,4},{12,6},{14,8},{1,11},{3,13... | collective-permute-start | bytes 1382408 | tf_op jit(solution)/shard_map/ppermute | solution.py:20
  145.4 16.0 %collective-permute-done.5 = bf16[150,1536]{1,0:T(8,128)(2,1)S(1)} collective-permute-done((bf16[150,1536]{1,0:T(8,128)(2,1)}, bf16[150,1536]{1,0:T(8,128)(2,1)S(1)}, u32[]{:S(2)}, u32[]{:S(2)}) %collective-permute-start.5) | collective-permute-done | bytes 460832 | tf_op jit(solution)/shard_map/ppermute | solution.py:20
  161.5 34.4 %concatenate.39 = bf16[1606,1536]{1,0:T(8,128)(2,1)} concatenate(bf16[150,1536]{1,0:T(8,128)(2,1)} %collective-permute-done, bf16[150,1536]{1,0:T(8,128)(2,1)} %collective-permute-done.1, bf16[150,1536]{1,0:T(8,128)(2,1)} %collective-permute-done.2, bf16[150,1536]{1,0:T(8,128)(2,1)} %collective-permute-done.2, bf16[150,1536]{1,0:T(8,128)(2,1)} %pad_maximum_fusion.1, ...), dimensions={0} | concatenate | bytes 9867264 | tf_op jit(solution)/shard_map/concatenate | solution.py:119
  195.9 1.6 fusion.55
  197.8 1.6 fusion.56
  199.7 1.7 fusion.57
  201.7 1.6 fusion.58
  203.5 1.6 fusion.59
  205.4 1.6 fusion.60
  209.9 22.8 %all-gather.2.cloned.1.call-done = bf16[768,3072]{1,0:T(8,128)(2,1)} async-done(((bf16[768,384]{1,0:T(8,128)(2,1)}), bf16[768,3072]{1,0:T(8,128)(2,1)}) %all-gather.2.cloned.1.call-update) | async-done | bytes 4718608 | tf_op jit(solution)/shard_map/all_gather | solution.py:144
  232.6 4.2 %convolution_convert_fusion = bf16[150,3072]{1,0:T(8,128)(2,1)} fusion(bf16[150,768]{1,0:T(8,128)(2,1)S(1)} %fusion.10, bf16[768,3072]{1,0:T(8,128)(2,1)} %all-gather.2.cloned.1.call-done), kind=kOutput, calls=%fused_computation | convolution fusion | flops 708249600 | bytes 5870592 | tf_op jit(solution)/shard_map/dot_general | solution.py:142
  236.8 8.8 %reduce-scatter.2.cloned.1.call-done = bf16[150,1536]{1,0:T(8,128)(2,1)} async-done(((bf16[150,3072]{1,0:T(8,128)(2,1)}), bf16[150,1536]{1,0:T(8,128)(2,1)}) %reduce-scatter.2.cloned.1.call-update) | async-done | bytes 460816 | tf_op jit(solution)/shard_map/reduce_scatter | solution.py:147
  (67 shorter events, 14.9 us)
Async XLA Ops:
  6.5 1.4 copy-start
  6.5 5.2 %copy-start.3 = (s32[8]{0:T(128)S(1)}, s32[8]{0:T(128)}, u32[]{:S(2)}) copy-start(s32[8]{0:T(128)} %param.15) | copy-start | bytes 100
  6.5 8.4 %copy-start.2 = (bf16[150,768]{1,0:T(8,128)(2,1)S(1)}, bf16[150,768]{1,0:T(8,128)(2,1)}, u32[]{:S(2)}) copy-start(bf16[150,768]{1,0:T(8,128)(2,1)} %param.8) | copy-start | bytes 691204
  6.5 131.5 %all-reduce.2.cloned.1.call-start = ((), (), s32[]{:S(2)}) async-start(), calls=%async_computation.1 | async-start | bytes 3145728 | tf_op jit(solution)/shard_map/psum | solution.py:101
  10.9 221.7 %all-gather.2.cloned.1.call-start = ((), (), s32[]{:S(2)}) async-start(), calls=%async_computation.2 | async-start | bytes 5308416 | tf_op jit(solution)/shard_map/all_gather | solution.py:144
  11.7 234.0 %reduce-scatter.2.cloned.1.call-start = ((), (), s32[]{:S(2)}) async-start(), calls=%async_computation.3 | async-start | bytes 1400832 | tf_op jit(solution)/shard_map/reduce_scatter | solution.py:147
  25.7 115.4 %collective-permute-start = (bf16[150,1536]{1,0:T(8,128)(2,1)}, bf16[150,1536]{1,0:T(8,128)(2,1)}, u32[]{:S(2)}, u32[]{:S(2)}) collective-permute-start(bf16[150,1536]{1,0:T(8,128)(2,1)} %pad_maximum_fusion.1), channel_id=1, source_target_pairs={{0,6},{2,8},{4,10},{6,12},{8,14},{10,0},{12,2},{14,4},{1,7},{3,9},... | collective-permute-start | bytes 1382408 | tf_op jit(solution)/shard_map/ppermute | solution.py:20
  29.7 115.7 %collective-permute-start.1 = (bf16[150,1536]{1,0:T(8,128)(2,1)}, bf16[150,1536]{1,0:T(8,128)(2,1)}, u32[]{:S(2)}, u32[]{:S(2)}) collective-permute-start(bf16[150,1536]{1,0:T(8,128)(2,1)} %pad_maximum_fusion.1), channel_id=1, source_target_pairs={{0,4},{2,6},{4,8},{6,10},{8,12},{10,14},{12,0},{14,2},{1,5},{3,7},... | collective-permute-start | bytes 1382408 | tf_op jit(solution)/shard_map/ppermute | solution.py:20
  31.3 114.1 %collective-permute-start.2 = (bf16[150,1536]{1,0:T(8,128)(2,1)}, bf16[150,1536]{1,0:T(8,128)(2,1)}, u32[]{:S(2)}, u32[]{:S(2)}) collective-permute-start(bf16[150,1536]{1,0:T(8,128)(2,1)} %pad_maximum_fusion.1), channel_id=1, source_target_pairs={{0,2},{2,4},{4,6},{6,8},{8,10},{10,12},{12,14},{14,0},{1,3},{3,5},... | collective-permute-start | bytes 1382408 | tf_op jit(solution)/shard_map/ppermute | solution.py:20
  32.8 112.6 %collective-permute-start.3 = (bf16[150,1536]{1,0:T(8,128)(2,1)}, bf16[150,1536]{1,0:T(8,128)(2,1)}, u32[]{:S(2)}, u32[]{:S(2)}) collective-permute-start(bf16[150,1536]{1,0:T(8,128)(2,1)} %pad_maximum_fusion.1), channel_id=1, source_target_pairs={{0,14},{2,0},{4,2},{6,4},{8,6},{10,8},{12,10},{14,12},{1,15},{3,1}... | collective-permute-start | bytes 1382408 | tf_op jit(solution)/shard_map/ppermute | solution.py:20
  36.0 109.4 %collective-permute-start.4 = (bf16[150,1536]{1,0:T(8,128)(2,1)}, bf16[150,1536]{1,0:T(8,128)(2,1)}, u32[]{:S(2)}, u32[]{:S(2)}) collective-permute-start(bf16[150,1536]{1,0:T(8,128)(2,1)} %pad_maximum_fusion.1), channel_id=1, source_target_pairs={{0,12},{2,14},{4,0},{6,2},{8,4},{10,6},{12,8},{14,10},{1,13},{3,15... | collective-permute-start | bytes 1382408 | tf_op jit(solution)/shard_map/ppermute | solution.py:20
  141.2 20.3 %collective-permute-start.5 = (bf16[150,1536]{1,0:T(8,128)(2,1)}, bf16[150,1536]{1,0:T(8,128)(2,1)S(1)}, u32[]{:S(2)}, u32[]{:S(2)}) collective-permute-start(bf16[150,1536]{1,0:T(8,128)(2,1)} %pad_maximum_fusion.1), channel_id=1, source_target_pairs={{0,10},{2,12},{4,14},{6,0},{8,2},{10,4},{12,6},{14,8},{1,11},{3,13... | collective-permute-start | bytes 1382408 | tf_op jit(solution)/shard_map/ppermute | solution.py:20
  199.6 7.7 %copy-start.1 = (bf16[1606,1536]{1,0:T(8,128)(2,1)S(1)}, bf16[1606,1536]{1,0:T(8,128)(2,1)}, u32[]{:S(2)}) copy-start(bf16[1606,1536]{1,0:T(8,128)(2,1)} %concatenate.39) | copy-start | bytes 14800900
Sparse Core Ops, SparseCore 0:
  11.1 126.9 all-reduce.1
  140.1 92.4 all-gather.1
  237.0 8.6 reduce-scatter.1
where the time goes:
time: 254 us; the launch traced here: 252 us
  waiting for transfers between devices  140 us (55%)
  local copies, waits for them, and re-layouts  44.1 us (17%)
  between operations  22.3 us (9%)
  matrix products  19.3 us (8%)
  starting transfers between devices  13.8 us (5%)
  other arithmetic  12.8 us (5%)
    psum x1, waiting for transfers between devices, body(): summed_text = lax.psum(partial_text, 'space')  91.5 us
    concatenate x1, local copies, waits for them, and re-layouts, body(): keys_all = jnp.concatenate(blocks, axis=0)  34.4 us
    all_gather x1, waiting for transfers between devices, body(): lax.all_gather(out_weight, 'space', axis=1, tiled=True)  22.8 us
    ppermute x6, waiting for transfers between devices, shifted(): return lax.ppermute(value, axis, pairs)  16.1 us
    ppermute x6, starting transfers between devices, shifted(): return lax.ppermute(value, axis, pairs)  13.7 us
    dot_general x6, matrix products, body(): lax.dot_general(query_slice, key_slice, (((1,), (1,)), ((), ())), preferr...  9.63 us
    reduce_scatter x1, waiting for transfers between devices, body(): lax.psum_scatter(partial_out.astype(jnp.bfloat16), 'heads', scatter_dimen...  8.8 us
  transfers between devices with their start and end apart: 9, of which 4 were waited for; matrix products, arithmetic and copies ran while one was open for 27% of the time, Pallas kernels for 0%

commit v1 on v0

--- a/solution.py
+++ b/solution.py
@@ -1,6 +1,11 @@
+import functools
+
 import jax
 import jax.numpy as jnp
+import numpy as np
 from jax import lax
+from jax.experimental import pallas as pl
+from jax.experimental.pallas import tpu as pltpu
 from jax.sharding import PartitionSpec as P
 
 HD = 128
@@ -150,6 +155,307 @@
     return summed_out
 
 
+MESH = pl.DeviceIdType.MESH
+
+
+def mult(value, step):
+    return pl.multiple_of(value, step)
+
+
+def fused_kernel(
+    rows,
+    head_count,
+    rope_ref,
+    bias_ref,
+    qkv_ref,
+    prompt_ref,
+    kw_ref,
+    vw_ref,
+    ow_ref,
+    out_ref,
+    tcols,
+    xs_q,
+    xs_kv,
+    qbuf,
+    kv,
+    txs,
+    txr,
+    tsum,
+    rss,
+    rsr,
+    att_s,
+    att,
+    wbuf,
+    part_s,
+    part_r,
+    local_sem,
+    send_sem,
+    recv_sem,
+):
+    g = lax.axis_index("groups")
+    s = lax.axis_index("space")
+    h = lax.axis_index("heads")
+    a, b = s // 2, s % 2
+    other = 1 - b
+    half = head_count // 2
+    width = half * HD
+    full = head_count * HD
+    x_peer = {"space": a * 2 + other}
+    y_peer = {"groups": 1 - g}
+    core_peer = {"heads": 1 - h}
+    z_row = [lax.rem(a + d, 4) for d in range(4)]
+    z_from = [lax.rem(a + 4 - d, 4) for d in range(4)]
+    z_peer = [{"space": z_row[d] * 2 + b} for d in range(4)]
+    kdim = kw_ref.shape[0]
+    text = tsum.shape[0]
+    piece = text // 4
+    text_at = 6 * rows
+
+    fetch = pltpu.make_async_copy(
+        prompt_ref.at[:, pl.ds(mult(s * kdim, 128), kdim)], tcols, local_sem.at[0]
+    )
+    fetch.start()
+
+    barrier = pltpu.get_barrier_semaphore()
+    peers = [x_peer, y_peer, core_peer, z_peer[1], z_peer[2], z_peer[3]]
+    for peer in peers:
+        pl.semaphore_signal(barrier, inc=1, device_id=peer, device_id_type=MESH)
+
+    started = []
+
+    def send(source, target, peer):
+        index = len(started)
+        copy = pltpu.make_async_remote_copy(
+            src_ref=source,
+            dst_ref=target,
+            send_sem=send_sem.at[index],
+            recv_sem=recv_sem.at[index],
+            device_id=peer,
+            device_id_type=MESH,
+        )
+        copy.start()
+        started.append(copy)
+        return copy
+
+    def turned(column):
+        x = qkv_ref[:, pl.ds(mult(column, 128), HD)].astype(jnp.float32)
+        lane = lax.broadcasted_iota(jnp.int32, x.shape, 1)
+        swapped = jnp.where(lane % 2 == 0, pltpu.roll(x, HD - 1, 1), pltpu.roll(x, 1, 1))
+        return (x * rope_ref[0] + swapped * rope_ref[1]).astype(jnp.bfloat16)
+
+    def seg(row, tile):
+        return pl.ds(mult((row * 2 + tile) * rows, 16), rows)
+
+    for m in range(half):
+        place = slice(m * HD, (m + 1) * HD)
+        xs_kv[:, place] = turned(full + other * width + m * HD)
+        xs_q[:, place] = turned(other * width + m * HD)
+        kv[seg(0, b), place] = turned(full + b * width + m * HD)
+    xs_kv[:, width:] = qkv_ref[:, pl.ds(mult(2 * full + other * width, 128), width)]
+    kv[seg(0, b), width:] = qkv_ref[:, pl.ds(mult(2 * full + b * width, 128), width)]
+
+    pl.semaphore_wait(barrier, len(peers))
+
+    def text_part(which):
+        cols = pl.ds(mult(which * width, 128), width)
+        return [
+            jnp.dot(tcols[...], w[:, cols], preferred_element_type=jnp.float32)
+            for w in (kw_ref, vw_ref)
+        ]
+
+    x_kv = send(xs_kv, kv.at[seg(0, b)], x_peer)
+    z_kv = [
+        send(kv.at[seg(0, b)], kv.at[seg(1, b)], z_peer[1]),
+        send(kv.at[seg(0, b)], kv.at[seg(2, b)], z_peer[3]),
+    ]
+    fetch.wait()
+    key_part, value_part = text_part(other)
+    txs[:, :width] = key_part.astype(jnp.bfloat16)
+    txs[:, width:] = value_part.astype(jnp.bfloat16)
+    x_text = send(txs, txr, x_peer)
+    x_q = send(xs_q, qbuf.at[b], x_peer)
+
+    mine = pl.ds(mult(g * width, 16), width)
+    z_w = [send(ow_ref.at[mine], wbuf.at[s, mine], z_peer[d]) for d in (1, 2, 3)]
+    x_w = [send(ow_ref.at[mine], wbuf.at[s, mine], x_peer)]
+
+    key_part, value_part = text_part(b)
+    tsum[:, :width] = key_part
+    tsum[:, width:] = value_part
+    for m in range(half):
+        qbuf[b, :, m * HD : (m + 1) * HD] = turned(b * width + m * HD)
+    wbuf[s] = ow_ref[...]
+
+    x_kv.wait_recv()
+    z_kv += [
+        send(kv.at[seg(0, other)], kv.at[seg(1, other)], z_peer[1]),
+        send(kv.at[seg(0, other)], kv.at[seg(2, other)], z_peer[3]),
+    ]
+
+    x_text.wait_recv()
+    z_text = []
+    for d in (1, 2, 3):
+        block = pl.ds(mult(z_row[d] * piece, 16), piece)
+        rss[d - 1] = (tsum[block, :] + txr[block, :].astype(jnp.float32)).astype(jnp.bfloat16)
+        z_text.append(send(rss.at[d - 1], rsr.at[d - 1], z_peer[d]))
+    block = pl.ds(mult(a * piece, 16), piece)
+    total = tsum[block, :] + txr[block, :].astype(jnp.float32)
+    for d in (1, 2, 3):
+        z_text[d - 1].wait_recv()
+        total = total + rsr[d - 1].astype(jnp.float32)
+    own_text = pl.ds(mult(text_at + a * piece, 16), piece)
+    for m in range(half):
+        x = total[:, m * HD : (m + 1) * HD]
+        x = x * lax.rsqrt(jnp.mean(x * x, axis=-1, keepdims=True) + eps_norm)
+        kv[own_text, m * HD : (m + 1) * HD] = x.astype(jnp.bfloat16)
+    kv[own_text, width:] = total[:, width:].astype(jnp.bfloat16)
+    z_text_kv = [send(kv.at[own_text], kv.at[own_text], z_peer[d]) for d in (1, 2, 3)]
+
+    y_w = []
+    for d in (1, 2, 3):
+        z_w[d - 1].wait_recv()
+        chunk = wbuf.at[z_from[d] * 2 + b, mine]
+        x_w.append(send(chunk, chunk, x_peer))
+        y_w.append(send(chunk, chunk, y_peer))
+    for d in range(4):
+        x_w[d].wait_recv()
+        chunk = wbuf.at[z_from[d] * 2 + other, mine]
+        y_w.append(send(chunk, chunk, y_peer))
+
+    for copy in [x_q] + z_kv + z_text_kv:
+        copy.wait_recv()
+
+    bias = bias_ref[...]
+    for tile in (other, b):
+        for m in range(half):
+            place = slice(m * HD, (m + 1) * HD)
+            scores = lax.dot_general(
+                qbuf[tile, :, place],
+                kv[:, place],
+                (((1,), (1,)), ((), ())),
+                preferred_element_type=jnp.float32,
+            )
+            scores = scores * HD ** (-0.5) + bias
+            top = jnp.max(scores, axis=-1, keepdims=True)
+            grown = jnp.exp(scores - top)
+            scaled = grown * (1.0 / jnp.sum(grown, axis=-1, keepdims=True))
+            result = jnp.dot(
+                scaled.astype(jnp.bfloat16),
+                kv[:, width + m * HD : width + (m + 1) * HD],
+                preferred_element_type=jnp.float32,
+            ).astype(jnp.bfloat16)
+            if tile is other:
+                att_s[:, place] = result
+            else:
+                att[:, pl.ds(mult(b * width + m * HD, 128), HD)] = result
+        if tile is other:
+            x_att = send(att_s, att.at[:, pl.ds(mult(b * width, 128), width)], x_peer)
+
+    for copy in y_w:
+        copy.wait_recv()
+    x_att.wait_recv()
+    cols = wbuf.shape[2]
+    for j in range(4):
+        part_s[:, j * cols : (j + 1) * cols] = jnp.dot(
+            att[...], wbuf[(1 - h) * 4 + j], preferred_element_type=jnp.float32
+        ).astype(jnp.bfloat16)
+    core = send(part_s, part_r, core_peer)
+    for j in range(4):
+        out_ref[:, j * cols : (j + 1) * cols] = jnp.dot(
+            att[...], wbuf[h * 4 + j], preferred_element_type=jnp.float32
+        ).astype(jnp.bfloat16)
+    core.wait_recv()
+    out_ref[...] = (
+        out_ref[...].astype(jnp.float32) + part_r[...].astype(jnp.float32)
+    ).astype(jnp.bfloat16)
+    for copy in started:
+        copy.wait_send()
+
+
+def rope_frequencies():
+    pair = np.arange(HD) // 2
+    time = np.where(pair < RT // 2, rope_theta ** (-2.0 * pair / RT), 0.0)
+    first = RT // 2
+    second = first + RH // 2
+    height = np.where(
+        (pair >= first) & (pair < second), rope_theta ** (-2.0 * (pair - first) / RH), 0.0
+    )
+    width = np.where(pair >= second, rope_theta ** (-2.0 * (pair - second) / RH), 0.0)
+    return [value.astype(np.float32)[None, :] for value in (time, height, width)]
+
+
+def fused_body(
+    queries, latent_keys, latent_values, prompt, key_weight, value_weight, out_weight, tile_owner
+):
+    device = lax.axis_index("space")
+    grid_h, grid_w = 4, 2
+    tok_rows = queries.shape[0]
+    full = queries.shape[1]
+    head_count = full // HD
+    width = full // 2
+    text = prompt.shape[0]
+    rows = -(-tok_rows // 16) * 16
+    tile_index = jnp.arange(tile_owner.shape[0], dtype=jnp.int32)
+    own_tile = jnp.sum(jnp.where(tile_owner == device, tile_index, 0))
+    tile_row = own_tile // grid_w
+    tile_col = own_tile % grid_w
+    row_sign = jnp.where(
+        (tile_owner[grid_w] // grid_w - tile_owner[0] // grid_w) % grid_h == 1, 1, -1
+    )
+    cell = jnp.arange(rows, dtype=jnp.int32)
+    frame_pos = (cell // (TILE * TILE)).astype(jnp.float32)[:, None]
+    height_pos = (tile_row * TILE + cell // TILE % TILE).astype(jnp.float32)[:, None]
+    width_pos = (tile_col * TILE + cell % TILE).astype(jnp.float32)[:, None]
+    time_freq, height_freq, width_freq = rope_frequencies()
+    angles = frame_pos * time_freq + height_pos * height_freq + width_pos * width_freq
+    sign = np.where(np.arange(HD) % 2 == 0, -1.0, 1.0).astype(np.float32)[None, :]
+    rope = jnp.stack([jnp.cos(angles), jnp.sin(angles) * sign])
+    step = np.repeat(np.array([0, -1, 1]), 2 * rows)
+    real = np.tile(np.arange(rows) < tok_rows, 6)
+    near = tile_row + row_sign * step
+    latent_bias = jnp.where((near >= 0) & (near < grid_h) & real, 0.0, masked_score)
+    bias = jnp.concatenate([latent_bias, jnp.zeros((text,))]).astype(jnp.float32)[None, :]
+    qkv = jnp.pad(
+        jnp.concatenate([queries, latent_keys, latent_values], axis=1),
+        ((0, rows - tok_rows), (0, 0)),
+    )
+    keys = 6 * rows + text
+    chunk = out_weight.shape
+    bf16 = jnp.bfloat16
+    vmem = pl.BlockSpec(memory_space=pltpu.VMEM)
+    copies = 32
+    result = pl.pallas_call(
+        functools.partial(fused_kernel, rows, head_count),
+        out_shape=jax.ShapeDtypeStruct((rows, 4 * chunk[1]), bf16),
+        in_specs=[vmem, vmem, vmem, pl.BlockSpec(memory_space=pl.ANY), vmem, vmem, vmem],
+        out_specs=vmem,
+        scratch_shapes=[
+            pltpu.VMEM((text, key_weight.shape[0]), bf16),
+            pltpu.VMEM((rows, width), bf16),
+            pltpu.VMEM((rows, full), bf16),
+            pltpu.VMEM((2, rows, width), bf16),
+            pltpu.VMEM((keys, full), bf16),
+            pltpu.VMEM((text, full), bf16),
+            pltpu.VMEM((text, full), bf16),
+            pltpu.VMEM((text, full), jnp.float32),
+            pltpu.VMEM((3, text // 4, full), bf16),
+            pltpu.VMEM((3, text // 4, full), bf16),
+            pltpu.VMEM((rows, width), bf16),
+            pltpu.VMEM((rows, full), bf16),
+            pltpu.VMEM((8,) + chunk, bf16),
+            pltpu.VMEM((rows, 4 * chunk[1]), bf16),
+            pltpu.VMEM((rows, 4 * chunk[1]), bf16),
+            pltpu.SemaphoreType.DMA((1,)),
+            pltpu.SemaphoreType.DMA((copies,)),
+            pltpu.SemaphoreType.DMA((copies,)),
+        ],
+        compiler_params=pltpu.CompilerParams(
+            collective_id=0, has_side_effects=True, vmem_limit_bytes=48 * 1024 * 1024
+        ),
+    )(rope, bias, qkv, prompt, key_weight, value_weight, out_weight)
+    return result[:tok_rows]
+
+
 def solution(mesh):
     in_specs = (
         P(("groups", "space"), "heads"),
@@ -162,4 +468,6 @@
         P("groups"),
     )
     out_specs = P(("groups", "space"), "heads")
-    return jax.shard_map(body, mesh=mesh, in_specs=in_specs, out_specs=out_specs, check_vma=False)
+    small = mesh.shape["space"] == 8 and mesh.shape["groups"] == 2 and mesh.shape["heads"] == 2
+    chosen = fused_body if small else body
+    return jax.shard_map(chosen, mesh=mesh, in_specs=in_specs, out_specs=out_specs, check_vma=False)

time: 254 us -> 126 us (0.50)
  waiting for transfers between devices: 140 us -> 0 us
  Pallas kernels: 0 us -> 107 us
  local copies, waits for them, and re-layouts: 44.1 us -> 5.33 us
  matrix products: 19.3 us -> 0 us
  between operations: 22.3 us -> 7.78 us
  starting transfers between devices: 13.8 us -> 0 us
  other arithmetic: 12.8 us -> 4.51 us
    pallas_call x0 -> x1, Pallas kernels: none -> 107 us  [fused_body(): pl.pallas_call(functools.partial(fused_kernel, rows, head_count), out_sha...]
    psum x1 -> x0, waiting for transfers between devices: 91.5 us -> none  [body(): summed_text = lax.psum(partial_text, 'space')]
    concatenate x2 -> x1, local copies, waits for them, and re-layouts: 34.5 us -> 0.01 us  [fused_body(): jnp.concatenate([latent_bias, jnp.zeros((text,))]).astype(jnp.float32)]
    all_gather x1 -> x0, waiting for transfers between devices: 22.8 us -> none  [body(): lax.all_gather(out_weight, 'space', axis=1, tiled=True)]
    dot_general x14 -> x0, matrix products: 19.3 us -> none  [the longest x6 9.63 us: body(): lax.dot_general(query_slice, key_slice, (((1,), (1,)), ((), ())), preferr...]
    ppermute x6 -> x0, waiting for transfers between devices: 16.1 us -> none  [shifted(): return lax.ppermute(value, axis, pairs)]
    ppermute x6 -> x0, starting transfers between devices: 13.7 us -> none  [shifted(): return lax.ppermute(value, axis, pairs)]
    reduce_scatter x1 -> x0, waiting for transfers between devices: 8.8 us -> none  [body(): lax.psum_scatter(partial_out.astype(jnp.bfloat16), 'heads', scatter_dimen...]
  transfers between devices with their start and end apart: 9 -> 0, of which waited for: 4 -> 0; matrix products, arithmetic and copies ran while one was open for 27% -> 0% of each run, Pallas kernels for 0% -> 0%
where the time goes in v1:
time: 126 us; the launch traced here: 125 us
  Pallas kernels  107 us (85%)
  between operations  7.78 us (6%)
  local copies, waits for them, and re-layouts  5.33 us (4%)
  other arithmetic  4.51 us (4%)
    pallas_call x1, Pallas kernels, fused_body(): pl.pallas_call(functools.partial(fused_kernel, rows, head_count), out_sha...  107 us
    unnamed x8, local copies, waits for them, and re-layouts  3.19 us

profile of v1, /device:TPU:0, one launch (start us, length us, event | category | flops | bytes accessed | tf_op | source)
XLA Modules:
  0.0 125.0 jit_solution(5625170433335663488)
XLA Ops:
  0.0 0.0 copy-start
  0.0 1.4 %fusion.19 = s32[]{:T(128)} fusion(s32[8]{0:T(128)} %param.21, s32[]{:T(128)S(6)} %axis_index.15), kind=kLoop, calls=%fused_computation.34 | loop fusion | flops 23 | bytes 40 | tf_op jit(solution)/shard_map/reduce_sum | solution.py:399
  4.1 1.3 %fusion.20 = (s32[1]{0:T(128)}, s32[1]{0:T(128)}) fusion(s32[8]{0:T(128)} %param.21), kind=kLoop, calls=%fused_computation.35 | loop fusion | bytes 16 | tf_op jit(solution)/shard_map/slice | solution.py:403
  10.5 0.7 fusion.10
  11.2 1.1 fusion.5
  12.4 1.2 fusion.4.qkv_ref
  13.6 0.0 copy-done
  13.6 0.0 copy-start.1
  13.6 1.1 copy-done.1
  14.7 0.0 copy-start.2
  14.7 1.1 copy-done.2
  15.7 0.0 copy-start.3
  15.7 1.1 copy-done.3
  16.8 107.4 %shard_map.136 = bf16[160,1536]{1,0:T(8,128)(2,1)S(1)} custom-call(f32[2,160,128]{2,1,0:T(8,128)S(1)} %pad_maximum_fusion.rope_ref, f32[1,1216]{1,0:T(1,128)S(1)} %broadcast_in_dim.22.bias_ref, bf16[160,2304]{1,0:T(8,128)(2,1)S(1)} %fusion.4.qkv_ref, bf16[256,3072]{1,0:T(8,128)(2,1)S(1)} %copy-done, bf16[384,768]{1,0:T(8,128)(2,1)S(1)} %copy-done.1, ...), custom_call_target="tpu_custom_call" | custom-call | tf_op jit(solution)/shard_map/pallas_call | solution.py:427
  124.2 0.8 slice.11
  (5 shorter events, 0.1 us)
Async XLA Ops:
  0.0 13.6 %copy-start = (bf16[256,3072]{1,0:T(8,128)(2,1)S(1)}, bf16[256,3072]{1,0:T(8,128)(2,1)}, u32[]{:S(2)}) copy-start(bf16[256,3072]{1,0:T(8,128)(2,1)} %prompt_ref.1) | copy-start | bytes 4718596
  13.6 1.1 copy-start.1
  14.7 1.1 copy-start.2
  15.7 1.1 copy-start.3

commit v2 on v1

--- a/solution.py
+++ b/solution.py
@@ -158,22 +158,33 @@
 MESH = pl.DeviceIdType.MESH
 
 
+UP_AT = 28
+DOWN_AT = 31
+ACROSS_AT = 34
+
+
 def mult(value, step):
     return pl.multiple_of(value, step)
 
 
 def fused_kernel(
     rows,
+    tok_rows,
     head_count,
-    rope_ref,
-    bias_ref,
-    qkv_ref,
+    owner_ref,
+    table_ref,
+    q_ref,
+    k_ref,
+    v_ref,
     prompt_ref,
-    kw_ref,
-    vw_ref,
+    kw_hbm,
+    vw_hbm,
     ow_ref,
     out_ref,
     tcols,
+    kw_ref,
+    vw_ref,
+    padded,
     xs_q,
     xs_kv,
     qbuf,
@@ -181,13 +192,17 @@
     txs,
     txr,
     tsum,
-    rss,
-    rsr,
-    att_s,
+    near_s,
+    near_r,
+    far_s,
+    far_r,
     att,
     wbuf,
     part_s,
     part_r,
+    kept,
+    swap_s,
+    swap_r,
     local_sem,
     send_sem,
     recv_sem,
@@ -203,10 +218,8 @@
     x_peer = {"space": a * 2 + other}
     y_peer = {"groups": 1 - g}
     core_peer = {"heads": 1 - h}
-    z_row = [lax.rem(a + d, 4) for d in range(4)]
-    z_from = [lax.rem(a + 4 - d, 4) for d in range(4)]
-    z_peer = [{"space": z_row[d] * 2 + b} for d in range(4)]
-    kdim = kw_ref.shape[0]
+    z_peer = [{"space": lax.rem(a + d, 4) * 2 + b} for d in range(4)]
+    kdim = kw_hbm.shape[0]
     text = tsum.shape[0]
     piece = text // 4
     text_at = 6 * rows
@@ -214,7 +227,16 @@
     fetch = pltpu.make_async_copy(
         prompt_ref.at[:, pl.ds(mult(s * kdim, 128), kdim)], tcols, local_sem.at[0]
     )
-    fetch.start()
+    fetches = [
+        fetch,
+        pltpu.make_async_copy(kw_hbm, kw_ref, local_sem.at[1]),
+        pltpu.make_async_copy(vw_hbm, vw_ref, local_sem.at[2]),
+    ]
+    own_w = pltpu.make_async_copy(
+        ow_ref.at[pl.ds(mult(b * width, 16), width)], wbuf.at[s], local_sem.at[3]
+    )
+    for copy in fetches + [own_w]:
+        copy.start()
 
     barrier = pltpu.get_barrier_semaphore()
     peers = [x_peer, y_peer, core_peer, z_peer[1], z_peer[2], z_peer[3]]
@@ -237,11 +259,36 @@
         started.append(copy)
         return copy
 
+    for part, ref in enumerate((q_ref, k_ref, v_ref)):
+        place = slice(part * full, (part + 1) * full)
+        padded[rows - 16 :, place] = jnp.zeros((16, full), jnp.float32)
+        padded[:tok_rows, place] = ref[...].astype(jnp.float32)
+
+    own_tile = jnp.int32(0)
+    for t in range(8):
+        own_tile = own_tile + jnp.where(owner_ref[t] == s, t, 0)
+    first_row, lower_row = owner_ref[0] // 2, owner_ref[2] // 2
+    row_sign = jnp.where(lax.rem(lower_row - first_row + 4, 4) == 1, 1, -1)
+    tile_row = own_tile // 2
+    one_hot = lax.broadcasted_iota(jnp.int32, (8, HD), 0) == own_tile
+    shift_cos, shift_sin = [
+        jnp.sum(
+            jnp.where(one_hot, table_ref[2 * rows + 8 * k : 2 * rows + 8 * k + 8], 0.0),
+            axis=0,
+            keepdims=True,
+        )
+        for k in range(2)
+    ]
+    base_cos, base_sin = table_ref[:rows], table_ref[rows : 2 * rows]
+    even = lax.broadcasted_iota(jnp.int32, (rows, HD), 1) % 2 == 0
+    cosine = base_cos * shift_cos - base_sin * shift_sin
+    sine = base_sin * shift_cos + base_cos * shift_sin
+    sine = jnp.where(even, -sine, sine)
+
     def turned(column):
-        x = qkv_ref[:, pl.ds(mult(column, 128), HD)].astype(jnp.float32)
-        lane = lax.broadcasted_iota(jnp.int32, x.shape, 1)
-        swapped = jnp.where(lane % 2 == 0, pltpu.roll(x, HD - 1, 1), pltpu.roll(x, 1, 1))
-        return (x * rope_ref[0] + swapped * rope_ref[1]).astype(jnp.bfloat16)
+        x = padded[:, pl.ds(mult(column, 128), HD)]
+        swapped = jnp.where(even, pltpu.roll(x, HD - 1, 1), pltpu.roll(x, 1, 1))
+        return (x * cosine + swapped * sine).astype(jnp.bfloat16)
 
     def seg(row, tile):
         return pl.ds(mult((row * 2 + tile) * rows, 16), rows)
@@ -251,8 +298,8 @@
         xs_kv[:, place] = turned(full + other * width + m * HD)
         xs_q[:, place] = turned(other * width + m * HD)
         kv[seg(0, b), place] = turned(full + b * width + m * HD)
-    xs_kv[:, width:] = qkv_ref[:, pl.ds(mult(2 * full + other * width, 128), width)]
-    kv[seg(0, b), width:] = qkv_ref[:, pl.ds(mult(2 * full + b * width, 128), width)]
+    xs_kv[:, width:] = padded[:, pl.ds(mult(2 * full + other * width, 128), width)].astype(jnp.bfloat16)
+    kv[seg(0, b), width:] = padded[:, pl.ds(mult(2 * full + b * width, 128), width)].astype(jnp.bfloat16)
 
     pl.semaphore_wait(barrier, len(peers))
 
@@ -268,23 +315,24 @@
         send(kv.at[seg(0, b)], kv.at[seg(1, b)], z_peer[1]),
         send(kv.at[seg(0, b)], kv.at[seg(2, b)], z_peer[3]),
     ]
-    fetch.wait()
+    for copy in fetches:
+        copy.wait()
     key_part, value_part = text_part(other)
     txs[:, :width] = key_part.astype(jnp.bfloat16)
     txs[:, width:] = value_part.astype(jnp.bfloat16)
     x_text = send(txs, txr, x_peer)
     x_q = send(xs_q, qbuf.at[b], x_peer)
 
-    mine = pl.ds(mult(g * width, 16), width)
-    z_w = [send(ow_ref.at[mine], wbuf.at[s, mine], z_peer[d]) for d in (1, 2, 3)]
-    x_w = [send(ow_ref.at[mine], wbuf.at[s, mine], x_peer)]
+    x_w = send(
+        ow_ref.at[pl.ds(mult(other * width, 16), width)], wbuf.at[s], x_peer
+    )
 
     key_part, value_part = text_part(b)
     tsum[:, :width] = key_part
     tsum[:, width:] = value_part
     for m in range(half):
         qbuf[b, :, m * HD : (m + 1) * HD] = turned(b * width + m * HD)
-    wbuf[s] = ow_ref[...]
+    own_w.wait()
 
     x_kv.wait_recv()
     z_kv += [
@@ -292,40 +340,111 @@
         send(kv.at[seg(0, other)], kv.at[seg(2, other)], z_peer[3]),
     ]
 
+    sub = width // 2
+    mine = pl.ds(mult(g * sub, 16), sub)
+
+    def row_of_chunks(row):
+        return wbuf.at[pl.ds(row * 2, 2), mine]
+
+    def copy_at(index, view, peer):
+        return pltpu.make_async_remote_copy(
+            src_ref=view,
+            dst_ref=view,
+            send_sem=send_sem.at[index],
+            recv_sem=recv_sem.at[index],
+            device_id=peer,
+            device_id_type=MESH,
+        )
+
+    up_peer = {"space": jnp.minimum(a + 1, 3) * 2 + b}
+    down_peer = {"space": jnp.maximum(a - 1, 0) * 2 + b}
+
+    def up_copy(k):
+        return copy_at(UP_AT + k, row_of_chunks(jnp.maximum(a - k, 0)), up_peer)
+
+    def down_copy(k):
+        return copy_at(DOWN_AT + k, row_of_chunks(jnp.minimum(a + k, 3)), down_peer)
+
+    def across_copy(d):
+        return copy_at(ACROSS_AT + d, row_of_chunks(lax.rem(a + d, 4)), y_peer)
+
+    def relay(k):
+        @pl.when(a >= k + 1)
+        def _():
+            up_copy(k).wait_recv()
+            across_copy(3 - k).start()
+
+        if k < 2:
+            @pl.when((a >= k + 1) & (a < 3))
+            def _():
+                up_copy(k + 1).start()
+
+        @pl.when(a <= 2 - k)
+        def _():
+            down_copy(k).wait_recv()
+            across_copy(1 + k).start()
+
+        if k < 2:
+            @pl.when((a <= 2 - k) & (a > 0))
+            def _():
+                down_copy(k + 1).start()
+
     x_text.wait_recv()
-    z_text = []
-    for d in (1, 2, 3):
-        block = pl.ds(mult(z_row[d] * piece, 16), piece)
-        rss[d - 1] = (tsum[block, :] + txr[block, :].astype(jnp.float32)).astype(jnp.bfloat16)
-        z_text.append(send(rss.at[d - 1], rsr.at[d - 1], z_peer[d]))
-    block = pl.ds(mult(a * piece, 16), piece)
-    total = tsum[block, :] + txr[block, :].astype(jnp.float32)
-    for d in (1, 2, 3):
-        z_text[d - 1].wait_recv()
-        total = total + rsr[d - 1].astype(jnp.float32)
-    own_text = pl.ds(mult(text_at + a * piece, 16), piece)
+    parity, upper = a % 2, a // 2
+    pair = 2 * piece
+    near_peer = {"space": (a + 1 - 2 * parity) * 2 + b}
+    far_peer = {"space": lax.rem(a + 2, 4) * 2 + b}
+    block = pl.ds(mult((1 - parity) * pair, 16), pair)
+    near_s[...] = (tsum[block, :] + txr[block, :].astype(jnp.float32)).astype(jnp.bfloat16)
+    near_text = send(near_s, near_r, near_peer)
+    block = pl.ds(mult(parity * pair, 16), pair)
+    tsum[block, :] = tsum[block, :] + txr[block, :].astype(jnp.float32)
+
+    x_w.wait_recv()
+
+    @pl.when(a < 3)
+    def _():
+        up_copy(0).start()
+
+    @pl.when(a > 0)
+    def _():
+        down_copy(0).start()
+
+    near_text.wait_recv()
+    lower_half = pl.ds(mult((1 - upper) * piece, 16), piece)
+    block = pl.ds(mult(parity * pair + (1 - upper) * piece, 16), piece)
+    far_s[...] = (tsum[block, :] + near_r[lower_half, :].astype(jnp.float32)).astype(jnp.bfloat16)
+    far_text = send(far_s, far_r, far_peer)
+    kept_half = pl.ds(mult(upper * piece, 16), piece)
+    block = pl.ds(mult(parity * pair + upper * piece, 16), piece)
+    total = tsum[block, :] + near_r[kept_half, :].astype(jnp.float32)
+    far_text.wait_recv()
+    total = total + far_r[...].astype(jnp.float32)
+    own_text = pl.ds(mult(text_at + parity * pair + upper * piece, 16), piece)
+    far_rows = pl.ds(mult(text_at + parity * pair + (1 - upper) * piece, 16), piece)
     for m in range(half):
         x = total[:, m * HD : (m + 1) * HD]
         x = x * lax.rsqrt(jnp.mean(x * x, axis=-1, keepdims=True) + eps_norm)
         kv[own_text, m * HD : (m + 1) * HD] = x.astype(jnp.bfloat16)
     kv[own_text, width:] = total[:, width:].astype(jnp.bfloat16)
-    z_text_kv = [send(kv.at[own_text], kv.at[own_text], z_peer[d]) for d in (1, 2, 3)]
-
-    y_w = []
-    for d in (1, 2, 3):
-        z_w[d - 1].wait_recv()
-        chunk = wbuf.at[z_from[d] * 2 + b, mine]
-        x_w.append(send(chunk, chunk, x_peer))
-        y_w.append(send(chunk, chunk, y_peer))
-    for d in range(4):
-        x_w[d].wait_recv()
-        chunk = wbuf.at[z_from[d] * 2 + other, mine]
-        y_w.append(send(chunk, chunk, y_peer))
-
+    far_kv = send(kv.at[own_text], kv.at[own_text], far_peer)
+    near_kv = send(kv.at[own_text], kv.at[own_text], near_peer)
+    far_kv.wait_recv()
+    near_kv2 = send(kv.at[far_rows], kv.at[far_rows], near_peer)
+
+    relay(0)
+    z_text_kv = [near_kv, near_kv2]
     for copy in [x_q] + z_kv + z_text_kv:
         copy.wait_recv()
 
-    bias = bias_ref[...]
+    key_at = lax.broadcasted_iota(jnp.int32, (1, kv.shape[0]), 1)
+    bias = jnp.where(key_at >= text_at, 0.0, masked_score)
+    for row, step in enumerate((0, -1, 1)):
+        near = tile_row + row_sign * step
+        level = jnp.where((near >= 0) & (near < 4), 0.0, masked_score)
+        for tile in range(2):
+            low = (row * 2 + tile) * rows
+            bias = jnp.where((key_at >= low) & (key_at < low + tok_rows), level, bias)
     for tile in (other, b):
         for m in range(half):
             place = slice(m * HD, (m + 1) * HD)
@@ -344,93 +463,92 @@
                 kv[:, width + m * HD : width + (m + 1) * HD],
                 preferred_element_type=jnp.float32,
             ).astype(jnp.bfloat16)
-            if tile is other:
-                att_s[:, place] = result
-            else:
-                att[:, pl.ds(mult(b * width + m * HD, 128), HD)] = result
-        if tile is other:
-            x_att = send(att_s, att.at[:, pl.ds(mult(b * width, 128), width)], x_peer)
-
-    for copy in y_w:
-        copy.wait_recv()
-    x_att.wait_recv()
+            att[pl.ds(mult(tile * rows, 16), rows), place] = result
+        relay(1 if tile is other else 2)
+
+    for d in (1, 2, 3):
+        across_copy(d).wait_recv()
     cols = wbuf.shape[2]
+    core = []
     for j in range(4):
-        part_s[:, j * cols : (j + 1) * cols] = jnp.dot(
+        part_s[j] = jnp.dot(
             att[...], wbuf[(1 - h) * 4 + j], preferred_element_type=jnp.float32
         ).astype(jnp.bfloat16)
-    core = send(part_s, part_r, core_peer)
+        core.append(send(part_s.at[j], part_r.at[j], core_peer))
     for j in range(4):
-        out_ref[:, j * cols : (j + 1) * cols] = jnp.dot(
-            att[...], wbuf[h * 4 + j], preferred_element_type=jnp.float32
+        kept[j] = jnp.dot(att[...], wbuf[h * 4 + j], preferred_element_type=jnp.float32)
+    sent_rows = pl.ds(mult(other * rows, 16), rows)
+    own_rows = pl.ds(mult(b * rows, 16), rows)
+    swap = []
+    for j in range(4):
+        core[j].wait_recv()
+        swap_s[j] = (
+            kept[j, sent_rows, :] + part_r[j, sent_rows, :].astype(jnp.float32)
         ).astype(jnp.bfloat16)
-    core.wait_recv()
-    out_ref[...] = (
-        out_ref[...].astype(jnp.float32) + part_r[...].astype(jnp.float32)
-    ).astype(jnp.bfloat16)
+        swap.append(send(swap_s.at[j], swap_r.at[j], x_peer))
+    for j in range(4):
+        total = kept[j, own_rows, :] + part_r[j, own_rows, :].astype(jnp.float32)
+        swap[j].wait_recv()
+        out_ref[:, j * cols : (j + 1) * cols] = (
+            total + swap_r[j].astype(jnp.float32)
+        ).astype(jnp.bfloat16)
+
     for copy in started:
         copy.wait_send()
-
-
-def rope_frequencies():
+    for d in (1, 2, 3):
+        across_copy(d).wait_send()
+    for k in range(3):
+        @pl.when((a >= k) & (a < 3))
+        def _():
+            up_copy(k).wait_send()
+
+        @pl.when((a <= 3 - k) & (a > 0))
+        def _():
+            down_copy(k).wait_send()
+
+
+def rope_constants(rows):
     pair = np.arange(HD) // 2
-    time = np.where(pair < RT // 2, rope_theta ** (-2.0 * pair / RT), 0.0)
     first = RT // 2
     second = first + RH // 2
-    height = np.where(
-        (pair >= first) & (pair < second), rope_theta ** (-2.0 * (pair - first) / RH), 0.0
-    )
+    in_height = (pair >= first) & (pair < second)
+    time = np.where(pair < first, rope_theta ** (-2.0 * pair / RT), 0.0)
+    height = np.where(in_height, rope_theta ** (-2.0 * (pair - first) / RH), 0.0)
     width = np.where(pair >= second, rope_theta ** (-2.0 * (pair - second) / RH), 0.0)
-    return [value.astype(np.float32)[None, :] for value in (time, height, width)]
+    cell = np.arange(rows)[:, None]
+    base = cell // (TILE * TILE) * time + cell // TILE % TILE * height + cell % TILE * width
+    tile = np.arange(8)[:, None]
+    shift = tile // 2 * TILE * height + tile % 2 * TILE * width
+    tables = [np.cos(base), np.sin(base), np.cos(shift), np.sin(shift)]
+    return np.concatenate(tables).astype(np.float32)
 
 
 def fused_body(
     queries, latent_keys, latent_values, prompt, key_weight, value_weight, out_weight, tile_owner
 ):
-    device = lax.axis_index("space")
-    grid_h, grid_w = 4, 2
     tok_rows = queries.shape[0]
     full = queries.shape[1]
     head_count = full // HD
     width = full // 2
     text = prompt.shape[0]
     rows = -(-tok_rows // 16) * 16
-    tile_index = jnp.arange(tile_owner.shape[0], dtype=jnp.int32)
-    own_tile = jnp.sum(jnp.where(tile_owner == device, tile_index, 0))
-    tile_row = own_tile // grid_w
-    tile_col = own_tile % grid_w
-    row_sign = jnp.where(
-        (tile_owner[grid_w] // grid_w - tile_owner[0] // grid_w) % grid_h == 1, 1, -1
-    )
-    cell = jnp.arange(rows, dtype=jnp.int32)
-    frame_pos = (cell // (TILE * TILE)).astype(jnp.float32)[:, None]
-    height_pos = (tile_row * TILE + cell // TILE % TILE).astype(jnp.float32)[:, None]
-    width_pos = (tile_col * TILE + cell % TILE).astype(jnp.float32)[:, None]
-    time_freq, height_freq, width_freq = rope_frequencies()
-    angles = frame_pos * time_freq + height_pos * height_freq + width_pos * width_freq
-    sign = np.where(np.arange(HD) % 2 == 0, -1.0, 1.0).astype(np.float32)[None, :]
-    rope = jnp.stack([jnp.cos(angles), jnp.sin(angles) * sign])
-    step = np.repeat(np.array([0, -1, 1]), 2 * rows)
-    real = np.tile(np.arange(rows) < tok_rows, 6)
-    near = tile_row + row_sign * step
-    latent_bias = jnp.where((near >= 0) & (near < grid_h) & real, 0.0, masked_score)
-    bias = jnp.concatenate([latent_bias, jnp.zeros((text,))]).astype(jnp.float32)[None, :]
-    qkv = jnp.pad(
-        jnp.concatenate([queries, latent_keys, latent_values], axis=1),
-        ((0, rows - tok_rows), (0, 0)),
-    )
     keys = 6 * rows + text
     chunk = out_weight.shape
     bf16 = jnp.bfloat16
     vmem = pl.BlockSpec(memory_space=pltpu.VMEM)
-    copies = 32
+    smem = pl.BlockSpec(memory_space=pltpu.SMEM)
+    hbm = pl.BlockSpec(memory_space=pltpu.HBM)
+    copies = 40
     result = pl.pallas_call(
-        functools.partial(fused_kernel, rows, head_count),
+        functools.partial(fused_kernel, rows, tok_rows, head_count),
         out_shape=jax.ShapeDtypeStruct((rows, 4 * chunk[1]), bf16),
-        in_specs=[vmem, vmem, vmem, pl.BlockSpec(memory_space=pl.ANY), vmem, vmem, vmem],
+        in_specs=[smem, vmem, vmem, vmem, vmem, hbm, hbm, hbm, hbm],
         out_specs=vmem,
         scratch_shapes=[
             pltpu.VMEM((text, key_weight.shape[0]), bf16),
+            pltpu.VMEM(key_weight.shape, bf16),
+            pltpu.VMEM(key_weight.shape, bf16),
+            pltpu.VMEM((rows, 3 * full), jnp.float32),
             pltpu.VMEM((rows, width), bf16),
             pltpu.VMEM((rows, full), bf16),
             pltpu.VMEM((2, rows, width), bf16),
@@ -438,21 +556,35 @@
             pltpu.VMEM((text, full), bf16),
             pltpu.VMEM((text, full), bf16),
             pltpu.VMEM((text, full), jnp.float32),
-            pltpu.VMEM((3, text // 4, full), bf16),
-            pltpu.VMEM((3, text // 4, full), bf16),
-            pltpu.VMEM((rows, width), bf16),
-            pltpu.VMEM((rows, full), bf16),
-            pltpu.VMEM((8,) + chunk, bf16),
-            pltpu.VMEM((rows, 4 * chunk[1]), bf16),
-            pltpu.VMEM((rows, 4 * chunk[1]), bf16),
-            pltpu.SemaphoreType.DMA((1,)),
+            pltpu.VMEM((text // 2, full), bf16),
+            pltpu.VMEM((text // 2, full), bf16),
+            pltpu.VMEM((text // 4, full), bf16),
+            pltpu.VMEM((text // 4, full), bf16),
+            pltpu.VMEM((2 * rows, width), bf16),
+            pltpu.VMEM((8, width, chunk[1]), bf16),
+            pltpu.VMEM((4, 2 * rows, chunk[1]), bf16),
+            pltpu.VMEM((4, 2 * rows, chunk[1]), bf16),
+            pltpu.VMEM((4, 2 * rows, chunk[1]), jnp.float32),
+            pltpu.VMEM((4, rows, chunk[1]), bf16),
+            pltpu.VMEM((4, rows, chunk[1]), bf16),
+            pltpu.SemaphoreType.DMA((4,)),
             pltpu.SemaphoreType.DMA((copies,)),
             pltpu.SemaphoreType.DMA((copies,)),
         ],
         compiler_params=pltpu.CompilerParams(
-            collective_id=0, has_side_effects=True, vmem_limit_bytes=48 * 1024 * 1024
+            collective_id=0, has_side_effects=True, vmem_limit_bytes=60 * 1024 * 1024
         ),
-    )(rope, bias, qkv, prompt, key_weight, value_weight, out_weight)
+    )(
+        tile_owner,
+        rope_constants(rows),
+        queries,
+        latent_keys,
+        latent_values,
+        prompt,
+        key_weight,
+        value_weight,
+        out_weight,
+    )
     return result[:tok_rows]
 
 

time: 126 us -> 87.3 us (0.69)
  Pallas kernels: 107 us -> 85.3 us
  between operations: 7.78 us -> 0.01 us
  other arithmetic: 4.51 us -> 0 us
  local copies, waits for them, and re-layouts: 5.33 us -> 1.82 us
    pallas_call x1, Pallas kernels: 107 us -> 85.3 us  [fused_body(): pl.pallas_call(functools.partial(fused_kernel, rows, tok_rows, head_count...]
    unnamed x8 -> x0, local copies, waits for them, and re-layouts: 3.19 us -> none
    reduce_sum x1 -> x0, other arithmetic: 1.41 us -> none  [fused_body(): own_tile = jnp.sum(jnp.where(tile_owner == device, tile_index, 0))]
    slice x1 -> x0, local copies, waits for them, and re-layouts: 1.32 us -> none  [fused_body(): tile_owner[0] // grid_w]
where the time goes in v2:
time: 87.3 us; the launch traced here: 87.1 us
  Pallas kernels  85.3 us (98%)
  local copies, waits for them, and re-layouts  1.82 us (2%)
    pallas_call x1, Pallas kernels, fused_body(): pl.pallas_call(functools.partial(fused_kernel, rows, tok_rows, head_count...  85.3 us
    slice x1, local copies, waits for them, and re-layouts, fused_body(): return result[:tok_rows]  1.82 us

profile of v2, /device:TPU:0, one launch (start us, length us, event | category | flops | bytes accessed | tf_op | source)
XLA Modules:
  0.0 87.1 jit_solution(3068275836640720)
XLA Ops:
  0.0 85.3 %shard_map.91 = bf16[160,1536]{1,0:T(8,128)(2,1)} custom-call(s32[8]{0:T(128)} %owner_ref.1, f32[336,128]{1,0:T(8,128)} %constant.2.clone.table_ref, bf16[150,768]{1,0:T(8,128)(2,1)} %q_ref.1, bf16[150,768]{1,0:T(8,128)(2,1)} %k_ref.1, bf16[150,768]{1,0:T(8,128)(2,1)} %v_ref.1, bf16[256,3072]{1,0:T(8,128)(2,1)} %prompt_ref.1, bf16[384,768]{1,0:T(8,128)(2,1)} %kw_hbm.1, ...), custom_call_target="tpu_custom_call" | custom-call | tf_op jit(solution)/shard_map/pallas_call | solution.py:542
  85.3 1.8 %slice.3 = bf16[150,1536]{1,0:T(8,128)(2,1)} slice(bf16[160,1536]{1,0:T(8,128)(2,1)} %shard_map.91), slice={[0:150], [0:1536]} | slice | bytes 921600 | tf_op jit(solution)/shard_map/slice | solution.py:588

commit v3 on v2

--- a/solution.py
+++ b/solution.py
@@ -259,6 +259,26 @@
         started.append(copy)
         return copy
 
+    def text_part(which):
+        cols = pl.ds(mult(which * width, 128), width)
+        return [
+            jnp.dot(tcols[...], w[:, cols], preferred_element_type=jnp.float32)
+            for w in (kw_ref, vw_ref)
+        ]
+
+    for copy in fetches:
+        copy.wait()
+    key_part, value_part = text_part(other)
+    txs[:, :width] = key_part.astype(jnp.bfloat16)
+    txs[:, width:] = value_part.astype(jnp.bfloat16)
+    pl.semaphore_wait(barrier, len(peers))
+
+    x_text = send(txs, txr, x_peer)
+
+    x_w = send(
+        ow_ref.at[pl.ds(mult(other * width, 16), width)], wbuf.at[s], x_peer
+    )
+
     for part, ref in enumerate((q_ref, k_ref, v_ref)):
         place = slice(part * full, (part + 1) * full)
         padded[rows - 16 :, place] = jnp.zeros((16, full), jnp.float32)
@@ -301,31 +321,12 @@
     xs_kv[:, width:] = padded[:, pl.ds(mult(2 * full + other * width, 128), width)].astype(jnp.bfloat16)
     kv[seg(0, b), width:] = padded[:, pl.ds(mult(2 * full + b * width, 128), width)].astype(jnp.bfloat16)
 
-    pl.semaphore_wait(barrier, len(peers))
-
-    def text_part(which):
-        cols = pl.ds(mult(which * width, 128), width)
-        return [
-            jnp.dot(tcols[...], w[:, cols], preferred_element_type=jnp.float32)
-            for w in (kw_ref, vw_ref)
-        ]
-
     x_kv = send(xs_kv, kv.at[seg(0, b)], x_peer)
     z_kv = [
         send(kv.at[seg(0, b)], kv.at[seg(1, b)], z_peer[1]),
         send(kv.at[seg(0, b)], kv.at[seg(2, b)], z_peer[3]),
     ]
-    for copy in fetches:
-        copy.wait()
-    key_part, value_part = text_part(other)
-    txs[:, :width] = key_part.astype(jnp.bfloat16)
-    txs[:, width:] = value_part.astype(jnp.bfloat16)
-    x_text = send(txs, txr, x_peer)
     x_q = send(xs_q, qbuf.at[b], x_peer)
-
-    x_w = send(
-        ow_ref.at[pl.ds(mult(other * width, 16), width)], wbuf.at[s], x_peer
-    )
 
     key_part, value_part = text_part(b)
     tsum[:, :width] = key_part
@@ -429,10 +430,11 @@
     kv[own_text, width:] = total[:, width:].astype(jnp.bfloat16)
     far_kv = send(kv.at[own_text], kv.at[own_text], far_peer)
     near_kv = send(kv.at[own_text], kv.at[own_text], near_peer)
+    relay(0)
     far_kv.wait_recv()
     near_kv2 = send(kv.at[far_rows], kv.at[far_rows], near_peer)
 
-    relay(0)
+    relay(1)
     z_text_kv = [near_kv, near_kv2]
     for copy in [x_q] + z_kv + z_text_kv:
         copy.wait_recv()
@@ -464,7 +466,8 @@
                 preferred_element_type=jnp.float32,
             ).astype(jnp.bfloat16)
             att[pl.ds(mult(tile * rows, 16), rows), place] = result
-        relay(1 if tile is other else 2)
+        if tile is other:
+            relay(2)
 
     for d in (1, 2, 3):
         across_copy(d).wait_recv()

time: 87.3 us -> 96.2 us (1.10)
  Pallas kernels: 85.3 us -> 94.2 us
    pallas_call x1, Pallas kernels: 85.3 us -> 94.2 us  [fused_body(): pl.pallas_call(functools.partial(fused_kernel, rows, tok_rows, head_count...]
where the time goes in v3:
time: 96.2 us; the launch traced here: 96 us
  Pallas kernels  94.2 us (98%)
  local copies, waits for them, and re-layouts  1.82 us (2%)
    pallas_call x1, Pallas kernels, fused_body(): pl.pallas_call(functools.partial(fused_kernel, rows, tok_rows, head_count...  94.2 us

profile of v3, /device:TPU:0, one launch (start us, length us, event | category | flops | bytes accessed | tf_op | source)
XLA Modules:
  0.0 96.0 jit_solution(4717761743606531239)
XLA Ops:
  0.0 94.2 %shard_map.91 = bf16[160,1536]{1,0:T(8,128)(2,1)} custom-call(s32[8]{0:T(128)} %owner_ref.1, f32[336,128]{1,0:T(8,128)} %constant.2.clone.table_ref, bf16[150,768]{1,0:T(8,128)(2,1)} %q_ref.1, bf16[150,768]{1,0:T(8,128)(2,1)} %k_ref.1, bf16[150,768]{1,0:T(8,128)(2,1)} %v_ref.1, bf16[256,3072]{1,0:T(8,128)(2,1)} %prompt_ref.1, bf16[384,768]{1,0:T(8,128)(2,1)} %kw_hbm.1, ...), custom_call_target="tpu_custom_call" | custom-call | tf_op jit(solution)/shard_map/pallas_call | solution.py:545
  94.2 1.8 %slice.3 = bf16[150,1536]{1,0:T(8,128)(2,1)} slice(bf16[160,1536]{1,0:T(8,128)(2,1)} %shard_map.91), slice={[0:150], [0:1536]} | slice | bytes 921600 | tf_op jit(solution)/shard_map/slice | solution.py:591

commit v4 on v2

--- a/solution.py
+++ b/solution.py
@@ -321,12 +321,11 @@
     txs[:, :width] = key_part.astype(jnp.bfloat16)
     txs[:, width:] = value_part.astype(jnp.bfloat16)
     x_text = send(txs, txr, x_peer)
-    x_q = send(xs_q, qbuf.at[b], x_peer)
-
     x_w = send(
         ow_ref.at[pl.ds(mult(other * width, 16), width)], wbuf.at[s], x_peer
     )
 
+    x_q = send(xs_q, qbuf.at[b], x_peer)
     key_part, value_part = text_part(b)
     tsum[:, :width] = key_part
     tsum[:, width:] = value_part
@@ -433,6 +432,7 @@
     near_kv2 = send(kv.at[far_rows], kv.at[far_rows], near_peer)
 
     relay(0)
+    relay(1)
     z_text_kv = [near_kv, near_kv2]
     for copy in [x_q] + z_kv + z_text_kv:
         copy.wait_recv()
@@ -464,7 +464,8 @@
                 preferred_element_type=jnp.float32,
             ).astype(jnp.bfloat16)
             att[pl.ds(mult(tile * rows, 16), rows), place] = result
-        relay(1 if tile is other else 2)
+        if tile is other:
+            relay(2)
 
     for d in (1, 2, 3):
         across_copy(d).wait_recv()

time: 87.3 us -> 87.6 us (level)
  no operation moved by 1% of the time
where the time goes in v4:
time: 87.6 us; the launch traced here: 87.4 us
  Pallas kernels  85.6 us (98%)
  local copies, waits for them, and re-layouts  1.82 us (2%)
    pallas_call x1, Pallas kernels, fused_body(): pl.pallas_call(functools.partial(fused_kernel, rows, tok_rows, head_count...  85.6 us
    slice x1, local copies, waits for them, and re-layouts, fused_body(): return result[:tok_rows]  1.82 us

profile of v4, /device:TPU:0, one launch (start us, length us, event | category | flops | bytes accessed | tf_op | source)
XLA Modules:
  0.0 87.4 jit_solution(10765955583218984096)
XLA Ops:
  0.0 85.6 %shard_map.91 = bf16[160,1536]{1,0:T(8,128)(2,1)} custom-call(s32[8]{0:T(128)} %owner_ref.1, f32[336,128]{1,0:T(8,128)} %constant.2.clone.table_ref, bf16[150,768]{1,0:T(8,128)(2,1)} %q_ref.1, bf16[150,768]{1,0:T(8,128)(2,1)} %k_ref.1, bf16[150,768]{1,0:T(8,128)(2,1)} %v_ref.1, bf16[256,3072]{1,0:T(8,128)(2,1)} %prompt_ref.1, bf16[384,768]{1,0:T(8,128)(2,1)} %kw_hbm.1, ...), custom_call_target="tpu_custom_call" | custom-call | tf_op jit(solution)/shard_map/pallas_call | solution.py:543
  85.6 1.8 %slice.3 = bf16[150,1536]{1,0:T(8,128)(2,1)} slice(bf16[160,1536]{1,0:T(8,128)(2,1)} %shard_map.91), slice={[0:150], [0:1536]} | slice | bytes 921600 | tf_op jit(solution)/shard_map/slice | solution.py:589
